TPU v7x, 32 devices: a whole 2x2x4 slice. The times are simulated.
32 devices in a mesh: red: 4 (over y, x), rep: 8 (over z, core).
Axes of the slice: x: 2, y: 2, z: 4, core: 2. Of those that a mesh axis runs over, the one named last changes fastest.
Arguments:
- amplitudes: float32 [8, 32, 8192], P(None, 'rep', 'red'), may hold values from -6 to 6
- integrals: float32 [8, 2048, 8192], P(None, 'red', 'rep'), may hold values from -0.0625 to 0.0625
Outputs:
- ladder: float32 [8, 32, 2048], P(None, 'rep', 'red')
All inputs are finite; a program needn't handle non-finite values.
Results may differ from a plain program's by a relative error of at most 0.00007.
Values sent between devices are 32-bit elements; how exact they have to be, the bound alone decides.
A program may use at most 64 MiB of HBM per device.

v0:
```python
import jax
import jax.numpy as jnp
from jax import lax
from jax.sharding import PartitionSpec as P


def contract(rows_block, integrals):
    return jnp.einsum("gic,gac->gia", rows_block, integrals, precision=lax.Precision.HIGHEST)


def per_device(amplitudes, integrals):
    full_pairs = lax.all_gather(amplitudes, "red", axis=2, tiled=True)
    ordered = lax.all_to_all(full_pairs, "rep", split_axis=2, concat_axis=1, tiled=True)
    partial_value = contract(ordered, integrals)
    contracted = lax.psum_scatter(partial_value, "rep", scatter_dimension=1, tiled=True)
    return 0.5 * contracted


def solution(mesh):
    in_specs = (P(None, "rep", "red"), P(None, "red", "rep"))
    out_specs = P(None, "rep", "red")
    return jax.shard_map(
        per_device, mesh=mesh, in_specs=in_specs, out_specs=out_specs, check_vma=False
    )
```

profile of v0, /device:TPU:0, one launch (start us, length us, event | category | flops | bytes accessed | tf_op | source)
XLA Modules:
  0.0 202.7 jit_solution(1292638145365039989)
XLA Ops:
  6.5 0.0 all-gather.2.cloned.1.call-start
  6.5 1.8 copy.8
  8.3 0.0 all-gather.2.cloned.1.call-update
  8.4 0.0 reduce-scatter.2.cloned.1.call-start
  8.4 30.2 %all-gather.2.cloned.1.call-done = f32[8,4,8192]{2,0,1:T(8,128)} async-done(((f32[8,4,2048]{2,0,1:T(8,128)}), f32[8,4,8192]{2,0,1:T(8,128)}) %all-gather.2.cloned.1.call-update) | async-done | bytes 1048592 | tf_op jit(solution)/shard_map/all_gather | solution.py:12
  38.6 11.9 %copy.9 = f32[8,4,8192]{0,1,2:T(4,128)} copy(f32[8,4,8192]{2,0,1:T(8,128)} %all-gather.2.cloned.1.call-done) | data formatting | bytes 2097152 | tf_op jit(solution)/shard_map/all_gather | solution.py:12
  50.5 21.3 %reshape = f32[8,1,32768]{2,1,0:T(1,128)S(1)} reshape(f32[8192,4,8]{2,1,0:T(4,128)} %bitcast.6) | data formatting | bytes 2097152
  71.8 31.0 %all_to_all.18 = f32[8,1,32768]{2,1,0:T(1,128)S(1)} all-to-all(f32[8,1,32768]{2,1,0:T(1,128)S(1)} %reshape), channel_id=1, replica_groups=mesh['red'=4,'rep'=8] {'rep'}, dimensions={0} | all-to-all | bytes 2097152 | tf_op jit(solution)/shard_map/all_to_all | solution.py:13
  102.8 0.5 broadcast
  103.3 3.1 %reduce = f32[8,32768]{1,0:T(8,128)S(1)} reduce(f32[8,1,32768]{2,1,0:T(1,128)S(1)} %all_to_all.18, f32[]{:T(128)} %broadcast), dimensions={1}, to_apply=%all_to_all.13.reduce_sub_computation | reduce | bytes 2097156 | tf_op jit(solution)/shard_map/all_to_all | solution.py:13
  106.4 25.6 %reshape.1 = f32[8192,4,8]{2,1,0:T(4,128)} reshape(f32[8,32768]{1,0:T(8,128)S(1)} %reduce) | data formatting | bytes 2097152
  132.0 13.1 %copy.10 = f32[8,4,8,1024]{3,1,2,0:T(4,128)S(1)} copy(f32[8,4,8,1024]{0,1,3,2:T(4,128)} %bitcast.7) | data formatting | bytes 2097152 | tf_op jit(solution)/shard_map/all_to_all | solution.py:13
  145.1 0.4 all_to_all.16
  145.5 18.6 %fusion = f32[8,32,512]{2,1,0:T(8,128)S(1)} fusion(f32[8,32,1024]{2,1,0:T(8,128)S(1)} %all_to_all.16, f32[8,512,1024]{2,1,0:T(8,128)} %param.3), kind=kOutput, calls=%fused_computation.1 | convolution fusion | flops 1610612736 | bytes 18350080 | tf_op jit(solution)/shard_map/gic,gac->gia/dot_general | solution.py:8
  164.2 1.1 copy.11
  165.3 0.0 reduce-scatter.2.cloned.1.call-update
  165.3 29.0 %reduce-scatter.2.cloned.1.call-done = f32[8,4,512]{2,0,1:T(8,128)} async-done(((f32[8,32,512]{2,0,1:T(8,128)}), f32[8,4,512]{2,0,1:T(8,128)}) %reduce-scatter.2.cloned.1.call-update) | async-done | bytes 65552 | tf_op jit(solution)/shard_map/reduce_scatter | solution.py:15
  194.3 0.8 broadcast_multiply_fusion
  195.1 0.7 copy.12
Async XLA Ops:
  6.5 32.0 %all-gather.2.cloned.1.call-start = ((), (), s32[]{:S(2)}) async-start(), calls=%async_computation.2 | async-start | bytes 1310720 | tf_op jit(solution)/shard_map/all_gather | solution.py:12
  8.4 185.9 %reduce-scatter.2.cloned.1.call-start = ((), (), s32[]{:S(2)}) async-start(), calls=%async_computation.3 | async-start | bytes 589824 | tf_op jit(solution)/shard_map/reduce_scatter | solution.py:15
Sparse Core Ops, SparseCore 0:
  9.2 29.3 all-gather.1
  165.4 28.8 reduce-scatter.1
where the time goes:
time: 204 us; the launch traced here: 203 us
  local copies, waits for them, and re-layouts  76.4 us (37%)
  waiting for transfers between devices  59.2 us (29%)
  blocking collectives  31 us (15%)
  matrix products  18.6 us (9%)
  between operations  13.4 us (7%)
  other arithmetic  3.98 us (2%)
    unnamed x3, local copies, waits for them, and re-layouts  48.7 us
    all_to_all x1, blocking collectives, per_device(): lax.all_to_all(full_pairs, 'rep', split_axis=2, concat_axis=1, tiled=True)  31 us
    all_gather x1, waiting for transfers between devices, per_device(): full_pairs = lax.all_gather(amplitudes, 'red', axis=2, tiled=True)  30.2 us
    reduce_scatter x1, waiting for transfers between devices, per_device(): lax.psum_scatter(partial_value, 'rep', scatter_dimension=1, tiled=True)  29 us
    dot_general x1, matrix products, contract(): jnp.einsum('gic,gac->gia', rows_block, integrals, precision=lax.Precision...  18.6 us
    all_to_all x3, local copies, waits for them, and re-layouts, per_device(): lax.all_to_all(full_pairs, 'rep', split_axis=2, concat_axis=1, tiled=True)  14 us
    all_gather x1, local copies, waits for them, and re-layouts, per_device(): full_pairs = lax.all_gather(amplitudes, 'red', axis=2, tiled=True)  11.9 us
  transfers between devices with their start and end apart: 2, of which 2 were waited for; matrix products, arithmetic and copies ran while one was open for 0% of the time, Pallas kernels for 0%

commit v1 on v0

v1 whole, which is shorter than its diff:
```python
import functools

import jax
import jax.numpy as jnp
from jax import lax
from jax.experimental import pallas as pl
from jax.experimental.pallas import tpu as pltpu
from jax.sharding import PartitionSpec as P

MESH = pl.DeviceIdType.MESH


def contract(rows_block, integrals):
    return jnp.einsum("gic,gac->gia", rows_block, integrals, precision=lax.Precision.HIGHEST)


def per_device_collectives(amplitudes, integrals):
    full_pairs = lax.all_gather(amplitudes, "red", axis=2, tiled=True)
    ordered = lax.all_to_all(full_pairs, "rep", split_axis=2, concat_axis=1, tiled=True)
    partial_value = contract(ordered, integrals)
    contracted = lax.psum_scatter(partial_value, "rep", scatter_dimension=1, tiled=True)
    return 0.5 * contracted


def ladder_kernel(
    amp, integ, out,
    raw, high, low, buf, part, from_core, summed, from_z,
    raw_sem, scatter_send, scatter_recv, plane_send, plane_recv, diag_send, diag_recv,
    core_send, core_recv, z_send, z_recv,
):
    n_rep, rows, cols = buf.shape[1:]
    half = n_rep // 2
    r, p = lax.axis_index("red"), lax.axis_index("rep")
    z, c = p // 2, p % 2
    x, y = r % 2, r // 2
    x_nbr = (1 - x) + 2 * y
    y_nbr = x + 2 * (1 - y)
    diag = (1 - x) + 2 * (1 - y)
    order = [(r, 0), (r, 1), (x_nbr, 0), (y_nbr, 0), (x_nbr, 1), (y_nbr, 1), (diag, 0), (diag, 1)]
    sym = [2 * q + j for q, j in order]

    def load(t):
        return pltpu.make_async_copy(integ.at[sym[t]], raw.at[t], raw_sem.at[t])

    for t in range(8):
        load(t).start()

    barrier = pltpu.get_barrier_semaphore()
    on_own = z == r

    def greet(red, rep):
        pl.semaphore_signal(barrier, inc=1, device_id=(red, rep), device_id_type=MESH)

    for k in range(1, n_rep):
        greet(z, (p + k) % n_rep)

    @pl.when(jnp.logical_not(on_own))
    def _():
        greet(z, p)

    greet(x_nbr, p)
    greet(y_nbr, p)
    greet(r, 2 * z + (1 - c))
    for k in range(1, 4):
        greet(r, 2 * ((z + k) % 4) + c)

    @pl.when(on_own)
    def _():
        pl.semaphore_wait(barrier, 13)

    @pl.when(jnp.logical_not(on_own))
    def _():
        pl.semaphore_wait(barrier, 14)

    def scatter(j, k, h):
        q = (r + k) % 4
        g = 2 * q + j
        src = amp.at[g, :, pl.ds(h * cols, cols)]
        dst = buf.at[g, p]
        target = 2 * r + h
        remote = pltpu.make_async_remote_copy(
            src_ref=src, dst_ref=dst, send_sem=scatter_send.at[j, k, h], recv_sem=scatter_recv.at[j],
            device_id=(q, target), device_id_type=MESH,
        )
        local = pltpu.make_async_copy(src, dst, scatter_recv.at[j])
        mine = jnp.logical_and(on_own, c == h) if k == 0 else None
        return remote, local, mine

    def scatter_all(act):
        for j in range(2):
            for k in range(4):
                for h in range(2):
                    remote, local, mine = scatter(j, k, h)
                    if mine is None:
                        act(remote)
                    else:
                        pl.when(jnp.logical_not(mine))(functools.partial(act, remote))
                        if act is start:
                            pl.when(mine)(local.start)

    def start(copy):
        copy.start()

    def wait_send(copy):
        copy.wait_send()

    scatter_all(start)

    def plane(j, way):
        g = 2 * r + j
        return pltpu.make_async_remote_copy(
            src_ref=buf.at[g], dst_ref=buf.at[g], send_sem=plane_send.at[j, way], recv_sem=plane_recv.at[j, way],
            device_id=((x_nbr, y_nbr)[way], p), device_id_type=MESH,
        )

    def onward(j, way):
        g = 2 * (x_nbr, y_nbr)[way] + j
        piece = buf.at[g, pl.ds(way * half, half)]
        return pltpu.make_async_remote_copy(
            src_ref=piece, dst_ref=piece, send_sem=diag_send.at[j, way], recv_sem=diag_recv.at[j],
            device_id=((y_nbr, x_nbr)[way], p), device_id_type=MESH,
        )

    def arrived(sem, ref):
        pltpu.make_async_copy(ref, ref, sem).wait()

    def own(j):
        arrived(scatter_recv.at[j], buf.at[2 * r + j])
        plane(j, 0).start()
        plane(j, 1).start()

    def from_plane(j, way):
        arrived(plane_recv.at[j, way], buf.at[2 * (x_nbr, y_nbr)[way] + j])
        onward(j, way).start()

    def from_diag(j):
        arrived(diag_recv.at[j], buf.at[2 * diag + j])

    step = 64
    n_a = raw.shape[1]

    def split(t):
        load(t).wait()

        @pl.loop(0, n_a // step)
        def _(s):
            here = pl.ds(pl.multiple_of(s * step, step), step)
            value = raw[t, here, :]
            top = value.astype(jnp.bfloat16)
            high[t, here, :] = top
            low[t, here, :] = (value - top.astype(jnp.float32)).astype(jnp.bfloat16)

    dims = (((1,), (1,)), ((), ()))
    n_i = n_rep * rows

    def to_core(t):
        return pltpu.make_async_remote_copy(
            src_ref=part.at[t, 1 - c], dst_ref=from_core.at[t], send_sem=core_send.at[t], recv_sem=core_recv.at[t],
            device_id=(r, 2 * z + (1 - c)), device_id_type=MESH,
        )

    def multiply(t):
        g = sym[t]
        value = jnp.concatenate([buf[g, k] for k in range(n_rep)], axis=0)
        top = value.astype(jnp.bfloat16)
        rest = (value - top.astype(jnp.float32)).astype(jnp.bfloat16)
        both = lax.dot_general(
            jnp.concatenate([top, rest], axis=0), high[t], dims, preferred_element_type=jnp.float32
        )
        more = lax.dot_general(top, low[t], dims, preferred_element_type=jnp.float32)
        product = both[:n_i] + (both[n_i:] + more)
        for k in range(n_rep):
            part[t, k % 2, k // 2] = product[k * rows:(k + 1) * rows]
        to_core(t).start()

    def to_z(t, k):
        there = (z + k) % 4
        return pltpu.make_async_remote_copy(
            src_ref=summed.at[t, there], dst_ref=from_z.at[t, k - 1], send_sem=z_send.at[t, k - 1],
            recv_sem=z_recv.at[t], device_id=(r, 2 * there + c), device_id_type=MESH,
        )

    def send_z(t):
        to_core(t).wait_recv()
        summed[t] = part[t, c] + from_core[t]
        for k in range(1, 4):
            to_z(t, k).start()

    def finish(t):
        arrived(z_recv.at[t], from_z.at[t])
        total = (summed[t, z] + from_z[t, 0]) + (from_z[t, 1] + from_z[t, 2])
        out[sym[t]] = 0.5 * total

    split(0)
    split(1)
    own(0)
    split(2)
    split(3)
    own(1)
    multiply(0)
    multiply(1)
    split(4)
    from_plane(0, 0)
    from_plane(0, 1)
    send_z(0)
    send_z(1)
    multiply(2)
    multiply(3)
    split(5)
    from_plane(1, 0)
    from_plane(1, 1)
    send_z(2)
    send_z(3)
    multiply(4)
    multiply(5)
    split(6)
    split(7)
    send_z(4)
    send_z(5)
    from_diag(0)
    multiply(6)
    from_diag(1)
    multiply(7)
    send_z(6)
    for t in range(4):
        finish(t)
    send_z(7)
    for t in range(4, 8):
        finish(t)

    scatter_all(wait_send)
    for j in range(2):
        for way in range(2):
            plane(j, way).wait_send()
            onward(j, way).wait_send()
    for t in range(8):
        to_core(t).wait_send()
        for k in range(1, 4):
            to_z(t, k).wait_send()


def per_device_kernel(amplitudes, integrals):
    n_sym, rows, _ = amplitudes.shape
    _, n_a, cols = integrals.shape
    n_rep = 8
    f32, bf16 = jnp.float32, jnp.bfloat16
    dma = pltpu.SemaphoreType.DMA
    return pl.pallas_call(
        ladder_kernel,
        out_shape=jax.ShapeDtypeStruct((n_sym, rows, n_a), f32),
        in_specs=[pl.BlockSpec(memory_space=pl.ANY)] * 2,
        out_specs=pl.BlockSpec(memory_space=pltpu.VMEM),
        scratch_shapes=[
            pltpu.VMEM((n_sym, n_a, cols), f32),
            pltpu.VMEM((n_sym, n_a, cols), bf16),
            pltpu.VMEM((n_sym, n_a, cols), bf16),
            pltpu.VMEM((n_sym, n_rep, rows, cols), f32),
            pltpu.VMEM((n_sym, 2, n_rep // 2, rows, n_a), f32),
            pltpu.VMEM((n_sym, n_rep // 2, rows, n_a), f32),
            pltpu.VMEM((n_sym, n_rep // 2, rows, n_a), f32),
            pltpu.VMEM((n_sym, n_rep // 2 - 1, rows, n_a), f32),
            dma((8,)),
            dma((2, 4, 2)),
            dma((2,)),
            dma((2, 2)),
            dma((2, 2)),
            dma((2, 2)),
            dma((2,)),
            dma((8,)),
            dma((8,)),
            dma((8, 3)),
            dma((8,)),
        ],
        compiler_params=pltpu.CompilerParams(
            collective_id=0, has_side_effects=True, vmem_limit_bytes=48 * 2**20
        ),
        cost_estimate=pl.CostEstimate(
            flops=6 * n_sym * n_rep * rows * n_a * cols, bytes_accessed=integrals.size * 4, transcendentals=0
        ),
    )(amplitudes, integrals)


def solution(mesh):
    in_specs = (P(None, "rep", "red"), P(None, "red", "rep"))
    out_specs = P(None, "rep", "red")
    fits = mesh.shape["red"] == 4 and mesh.shape["rep"] == 8
    return jax.shard_map(
        per_device_kernel if fits else per_device_collectives,
        mesh=mesh, in_specs=in_specs, out_specs=out_specs, check_vma=False,
    )
```

time: 204 us -> 41.1 us (0.20)
  local copies, waits for them, and re-layouts: 76.4 us -> 1.58 us
  waiting for transfers between devices: 59.2 us -> 0 us
  Pallas kernels: 0 us -> 39.4 us
  blocking collectives: 31 us -> 0 us
  matrix products: 18.6 us -> 0 us
  between operations: 13.4 us -> 0.01 us
  other arithmetic: 3.98 us -> 0 us
    unnamed x3, local copies, waits for them, and re-layouts: 48.7 us -> 1.58 us
    pallas_call x0 -> x1, Pallas kernels: none -> 39.4 us  [per_device_kernel(): pl.pallas_call(ladder_kernel, out_shape=jax.ShapeDtypeStruct((n_sym, rows...]
    all_to_all x1 -> x0, blocking collectives: 31 us -> none  [per_device(): lax.all_to_all(full_pairs, 'rep', split_axis=2, concat_axis=1, tiled=True)]
    all_gather x1 -> x0, waiting for transfers between devices: 30.2 us -> none  [per_device(): full_pairs = lax.all_gather(amplitudes, 'red', axis=2, tiled=True)]
    reduce_scatter x1 -> x0, waiting for transfers between devices: 29 us -> none  [per_device(): lax.psum_scatter(partial_value, 'rep', scatter_dimension=1, tiled=True)]
    dot_general x1 -> x0, matrix products: 18.6 us -> none  [contract(): jnp.einsum('gic,gac->gia', rows_block, integrals, precision=lax.Precision...]
    all_to_all x3 -> x0, local copies, waits for them, and re-layouts: 14 us -> none  [per_device(): lax.all_to_all(full_pairs, 'rep', split_axis=2, concat_axis=1, tiled=True)]
    all_gather x1 -> x0, local copies, waits for them, and re-layouts: 11.9 us -> none  [per_device(): full_pairs = lax.all_gather(amplitudes, 'red', axis=2, tiled=True)]
  transfers between devices with their start and end apart: 2 -> 0, of which waited for: 2 -> 0; matrix products, arithmetic and copies ran while one was open for 0% -> 0% of each run, Pallas kernels for 0% -> 0%
where the time goes in v1:
time: 41.1 us; the launch traced here: 41 us
  Pallas kernels  39.4 us (96%)
  local copies, waits for them, and re-layouts  1.58 us (4%)
    pallas_call x1, Pallas kernels, per_device_kernel(): pl.pallas_call(ladder_kernel, out_shape=jax.ShapeDtypeStruct((n_sym, rows...  39.4 us
    unnamed x3, local copies, waits for them, and re-layouts  1.58 us

profile of v1, /device:TPU:0, one launch (start us, length us, event | category | flops | bytes accessed | tf_op | source)
XLA Modules:
  0.0 41.0 jit_solution(1879936539104352576)
XLA Ops:
  0.0 0.0 copy-start
  0.0 0.9 %copy-done = f32[8,4,2048]{2,1,0:T(4,128)S(1)} copy-done((f32[8,4,2048]{2,1,0:T(4,128)S(1)}, f32[8,4,2048]{2,1,0:T(4,128)}, u32[]{:S(2)}) %copy-start) | copy-done | bytes 262168
  1.0 39.4 %shard_map.28 = f32[8,4,512]{2,1,0:T(4,128)S(1)} custom-call(f32[8,4,2048]{2,1,0:T(4,128)S(1)} %copy-done, f32[8,512,1024]{2,1,0:T(8,128)} %integ.1), custom_call_target="tpu_custom_call" | custom-call | flops 805306368 | bytes 16777216 | tf_op jit(solution)/shard_map/pallas_call | solution.py:248
  40.4 0.6 %copy.4 = f32[8,4,512]{2,1,0:T(4,128)} copy(f32[8,4,512]{2,1,0:T(4,128)S(1)} %shard_map.28) | data formatting | bytes 131072
Async XLA Ops:
  0.0 0.9 %copy-start = (f32[8,4,2048]{2,1,0:T(4,128)S(1)}, f32[8,4,2048]{2,1,0:T(4,128)}, u32[]{:S(2)}) copy-start(f32[8,4,2048]{2,1,0:T(4,128)} %amp.1) | copy-start | bytes 786436

commit v2 on v1

--- a/solution.py
+++ b/solution.py
@@ -24,8 +24,8 @@
 
 def ladder_kernel(
     amp, integ, out,
-    raw, high, low, buf, part, from_core, summed, from_z,
-    raw_sem, scatter_send, scatter_recv, plane_send, plane_recv, diag_send, diag_recv,
+    raw, high, low, stage, buf, part, from_core, summed, from_z,
+    raw_sem, spread_send, spread_recv, column_send, column_recv, plane_send, plane_recv, diag_send, diag_recv,
     core_send, core_recv, z_send, z_recv,
 ):
     n_rep, rows, cols = buf.shape[1:]
@@ -46,57 +46,37 @@
         load(t).start()
 
     barrier = pltpu.get_barrier_semaphore()
-    on_own = z == r
-
-    def greet(red, rep):
-        pl.semaphore_signal(barrier, inc=1, device_id=(red, rep), device_id_type=MESH)
-
-    for k in range(1, n_rep):
-        greet(z, (p + k) % n_rep)
-
-    @pl.when(jnp.logical_not(on_own))
-    def _():
-        greet(z, p)
-
-    greet(x_nbr, p)
-    greet(y_nbr, p)
-    greet(r, 2 * z + (1 - c))
-    for k in range(1, 4):
-        greet(r, 2 * ((z + k) % 4) + c)
-
-    @pl.when(on_own)
-    def _():
-        pl.semaphore_wait(barrier, 13)
-
-    @pl.when(jnp.logical_not(on_own))
-    def _():
-        pl.semaphore_wait(barrier, 14)
-
-    def scatter(j, k, h):
-        q = (r + k) % 4
-        g = 2 * q + j
-        src = amp.at[g, :, pl.ds(h * cols, cols)]
-        dst = buf.at[g, p]
-        target = 2 * r + h
-        remote = pltpu.make_async_remote_copy(
-            src_ref=src, dst_ref=dst, send_sem=scatter_send.at[j, k, h], recv_sem=scatter_recv.at[j],
-            device_id=(q, target), device_id_type=MESH,
-        )
-        local = pltpu.make_async_copy(src, dst, scatter_recv.at[j])
-        mine = jnp.logical_and(on_own, c == h) if k == 0 else None
-        return remote, local, mine
-
-    def scatter_all(act):
-        for j in range(2):
-            for k in range(4):
-                for h in range(2):
-                    remote, local, mine = scatter(j, k, h)
-                    if mine is None:
-                        act(remote)
-                    else:
-                        pl.when(jnp.logical_not(mine))(functools.partial(act, remote))
-                        if act is start:
-                            pl.when(mine)(local.start)
+    peers = [(x_nbr, p), (y_nbr, p), (diag, p)] + [(r, (p + k) % n_rep) for k in range(1, n_rep)]
+    for peer in peers:
+        pl.semaphore_signal(barrier, inc=1, device_id=peer, device_id_type=MESH)
+    pl.semaphore_wait(barrier, len(peers))
+
+    near = [r, x_nbr, y_nbr, diag]
+
+    def spread(j, k):
+        return pltpu.make_async_remote_copy(
+            src_ref=amp.at[2 * near[k] + j], dst_ref=stage.at[j, k - 1], send_sem=spread_send.at[j, k - 1],
+            recv_sem=spread_recv.at[j, k - 1], device_id=(near[k], p), device_id_type=MESH,
+        )
+
+    def column(j, k, h, act):
+        here = pl.ds(h * cols, cols)
+        src = amp.at[2 * r + j, :, here] if k == 0 else stage.at[j, k - 1, :, here]
+        dst = buf.at[2 * r + j, p]
+        target = 2 * near[k] + h
+        mine = target == p
+
+        @pl.when(jnp.logical_not(mine))
+        def _():
+            act(pltpu.make_async_remote_copy(
+                src_ref=src, dst_ref=dst, send_sem=column_send.at[j, k, h], recv_sem=column_recv.at[j, z],
+                device_id=(r, target), device_id_type=MESH,
+            ))
+
+        if act is start:
+            @pl.when(mine)
+            def _():
+                pltpu.make_async_copy(src, dst, column_recv.at[j, z]).start()
 
     def start(copy):
         copy.start()
@@ -104,18 +84,32 @@
     def wait_send(copy):
         copy.wait_send()
 
-    scatter_all(start)
-
-    def plane(j, way):
-        g = 2 * r + j
-        return pltpu.make_async_remote_copy(
-            src_ref=buf.at[g], dst_ref=buf.at[g], send_sem=plane_send.at[j, way], recv_sem=plane_recv.at[j, way],
+    def column_all(j, k, act):
+        for h in range(2):
+            column(j, k, h, act)
+
+    for j in range(2):
+        for k in range(1, 4):
+            spread(j, k).start()
+    for j in range(2):
+        column_all(j, 0, start)
+
+    upper = z // 2
+    z_order = [z, 2 * upper + 1 - z % 2, 2 - upper, 3 - 3 * upper]
+
+    def plane(j, n, way):
+        piece = buf.at[2 * r + j, pl.ds(2 * z_order[n], 2)]
+        return pltpu.make_async_remote_copy(
+            src_ref=piece, dst_ref=piece, send_sem=plane_send.at[j, n, way], recv_sem=plane_recv.at[j, way, n // 2],
             device_id=((x_nbr, y_nbr)[way], p), device_id_type=MESH,
         )
 
+    def half_of(g, n):
+        first = upper if n == 0 else 1 - upper
+        return buf.at[g, pl.ds(first * half, half)]
+
     def onward(j, way):
-        g = 2 * (x_nbr, y_nbr)[way] + j
-        piece = buf.at[g, pl.ds(way * half, half)]
+        piece = half_of(2 * (x_nbr, y_nbr)[way] + j, way)
         return pltpu.make_async_remote_copy(
             src_ref=piece, dst_ref=piece, send_sem=diag_send.at[j, way], recv_sem=diag_recv.at[j],
             device_id=((y_nbr, x_nbr)[way], p), device_id_type=MESH,
@@ -124,14 +118,23 @@
     def arrived(sem, ref):
         pltpu.make_async_copy(ref, ref, sem).wait()
 
+    def relay(j):
+        for k in range(1, 4):
+            arrived(spread_recv.at[j, k - 1], stage.at[j, k - 1])
+            column_all(j, k, start)
+
     def own(j):
-        arrived(scatter_recv.at[j], buf.at[2 * r + j])
-        plane(j, 0).start()
-        plane(j, 1).start()
-
-    def from_plane(j, way):
-        arrived(plane_recv.at[j, way], buf.at[2 * (x_nbr, y_nbr)[way] + j])
-        onward(j, way).start()
+        for n in range(4):
+            arrived(column_recv.at[j, z_order[n]], buf.at[2 * r + j, pl.ds(2 * z_order[n], 2)])
+            plane(j, n, 0).start()
+            plane(j, n, 1).start()
+
+    def from_plane(j):
+        for n in range(2):
+            for way in range(2):
+                arrived(plane_recv.at[j, way, n], half_of(2 * (x_nbr, y_nbr)[way] + j, n))
+                if n == way:
+                    onward(j, way).start()
 
     def from_diag(j):
         arrived(diag_recv.at[j], buf.at[2 * diag + j])
@@ -191,6 +194,8 @@
         total = (summed[t, z] + from_z[t, 0]) + (from_z[t, 1] + from_z[t, 2])
         out[sym[t]] = 0.5 * total
 
+    relay(0)
+    relay(1)
     split(0)
     split(1)
     own(0)
@@ -200,15 +205,13 @@
     multiply(0)
     multiply(1)
     split(4)
-    from_plane(0, 0)
-    from_plane(0, 1)
+    from_plane(0)
     send_z(0)
     send_z(1)
     multiply(2)
     multiply(3)
     split(5)
-    from_plane(1, 0)
-    from_plane(1, 1)
+    from_plane(1)
     send_z(2)
     send_z(3)
     multiply(4)
@@ -228,10 +231,14 @@
     for t in range(4, 8):
         finish(t)
 
-    scatter_all(wait_send)
     for j in range(2):
+        for k in range(1, 4):
+            spread(j, k).wait_send()
+        for k in range(4):
+            column_all(j, k, wait_send)
         for way in range(2):
-            plane(j, way).wait_send()
+            for n in range(4):
+                plane(j, n, way).wait_send()
             onward(j, way).wait_send()
     for t in range(8):
         to_core(t).wait_send()
@@ -254,16 +261,19 @@
             pltpu.VMEM((n_sym, n_a, cols), f32),
             pltpu.VMEM((n_sym, n_a, cols), bf16),
             pltpu.VMEM((n_sym, n_a, cols), bf16),
+            pltpu.VMEM((2, 3, rows, amplitudes.shape[2]), f32),
             pltpu.VMEM((n_sym, n_rep, rows, cols), f32),
             pltpu.VMEM((n_sym, 2, n_rep // 2, rows, n_a), f32),
             pltpu.VMEM((n_sym, n_rep // 2, rows, n_a), f32),
             pltpu.VMEM((n_sym, n_rep // 2, rows, n_a), f32),
             pltpu.VMEM((n_sym, n_rep // 2 - 1, rows, n_a), f32),
             dma((8,)),
+            dma((2, 3)),
+            dma((2, 3)),
             dma((2, 4, 2)),
-            dma((2,)),
-            dma((2, 2)),
-            dma((2, 2)),
+            dma((2, 4)),
+            dma((2, 4, 2)),
+            dma((2, 2, 2)),
             dma((2, 2)),
             dma((2,)),
             dma((8,)),

time: 41.1 us -> 32.7 us (0.80)
  Pallas kernels: 39.4 us -> 31 us
    pallas_call x1, Pallas kernels: 39.4 us -> 31 us  [per_device_kernel(): pl.pallas_call(ladder_kernel, out_shape=jax.ShapeDtypeStruct((n_sym, rows...]
where the time goes in v2:
time: 32.7 us; the launch traced here: 32.6 us
  Pallas kernels  31 us (95%)
  local copies, waits for them, and re-layouts  1.58 us (5%)
    pallas_call x1, Pallas kernels, per_device_kernel(): pl.pallas_call(ladder_kernel, out_shape=jax.ShapeDtypeStruct((n_sym, rows...  31 us
    unnamed x3, local copies, waits for them, and re-layouts  1.58 us

profile of v2, /device:TPU:0, one launch (start us, length us, event | category | flops | bytes accessed | tf_op | source)
XLA Modules:
  0.0 32.6 jit_solution(9961884054228005625)
XLA Ops:
  0.0 0.0 copy-start
  0.0 0.9 %copy-done = f32[8,4,2048]{2,1,0:T(4,128)S(1)} copy-done((f32[8,4,2048]{2,1,0:T(4,128)S(1)}, f32[8,4,2048]{2,1,0:T(4,128)}, u32[]{:S(2)}) %copy-start) | copy-done | bytes 262168
  1.0 31.0 %shard_map.28 = f32[8,4,512]{2,1,0:T(4,128)S(1)} custom-call(f32[8,4,2048]{2,1,0:T(4,128)S(1)} %copy-done, f32[8,512,1024]{2,1,0:T(8,128)} %integ.1), custom_call_target="tpu_custom_call" | custom-call | flops 805306368 | bytes 16777216 | tf_op jit(solution)/shard_map/pallas_call | solution.py:255
  32.0 0.6 %copy.4 = f32[8,4,512]{2,1,0:T(4,128)} copy(f32[8,4,512]{2,1,0:T(4,128)S(1)} %shard_map.28) | data formatting | bytes 131072
Async XLA Ops:
  0.0 0.9 %copy-start = (f32[8,4,2048]{2,1,0:T(4,128)S(1)}, f32[8,4,2048]{2,1,0:T(4,128)}, u32[]{:S(2)}) copy-start(f32[8,4,2048]{2,1,0:T(4,128)} %amp.1) | copy-start | bytes 786436

commit v3 on v2

--- a/solution.py
+++ b/solution.py
@@ -26,7 +26,7 @@
     amp, integ, out,
     raw, high, low, stage, buf, part, from_core, summed, from_z,
     raw_sem, spread_send, spread_recv, column_send, column_recv, plane_send, plane_recv, diag_send, diag_recv,
-    core_send, core_recv, z_send, z_recv,
+    core_send, core_recv, z_send, z_recv, known,
 ):
     n_rep, rows, cols = buf.shape[1:]
     half = n_rep // 2
@@ -46,10 +46,54 @@
         load(t).start()
 
     barrier = pltpu.get_barrier_semaphore()
-    peers = [(x_nbr, p), (y_nbr, p), (diag, p)] + [(r, (p + k) % n_rep) for k in range(1, n_rep)]
-    for peer in peers:
-        pl.semaphore_signal(barrier, inc=1, device_id=peer, device_id_type=MESH)
-    pl.semaphore_wait(barrier, len(peers))
+    last = n_rep // 2 - 1
+    has_below, has_above = z > 0, z < last
+
+    def signal(sem, red, rep):
+        pl.semaphore_signal(sem, inc=1, device_id=(red, rep), device_id_type=MESH)
+
+    for red in (diag, x_nbr, y_nbr):
+        signal(barrier, red, p)
+    signal(barrier, r, 2 * z + (1 - c))
+
+    @pl.when(has_below)
+    def _():
+        for h in range(2):
+            signal(barrier, r, 2 * (z - 1) + h)
+
+    @pl.when(has_above)
+    def _():
+        for h in range(2):
+            signal(barrier, r, 2 * (z + 1) + h)
+
+    inner = jnp.logical_and(has_below, has_above)
+
+
+    @pl.when(inner)
+    def _():
+        pl.semaphore_wait(barrier, 8)
+
+    @pl.when(jnp.logical_not(inner))
+    def _():
+        pl.semaphore_wait(barrier, 6)
+
+    def tell(n):
+        @pl.when(has_below)
+        def _():
+            signal(known.at[n], r, p - 2)
+
+        @pl.when(has_above)
+        def _():
+            signal(known.at[n], r, p + 2)
+
+    def hear(n):
+        @pl.when(inner)
+        def _():
+            pl.semaphore_wait(known.at[n], 2)
+
+        @pl.when(jnp.logical_not(inner))
+        def _():
+            pl.semaphore_wait(known.at[n], 1)
 
     near = [r, x_nbr, y_nbr, diag]
 
@@ -91,8 +135,7 @@
     for j in range(2):
         for k in range(1, 4):
             spread(j, k).start()
-    for j in range(2):
-        column_all(j, 0, start)
+    tell(0)
 
     upper = z // 2
     z_order = [z, 2 * upper + 1 - z % 2, 2 - upper, 3 - 3 * upper]
@@ -123,18 +166,16 @@
             arrived(spread_recv.at[j, k - 1], stage.at[j, k - 1])
             column_all(j, k, start)
 
-    def own(j):
-        for n in range(4):
-            arrived(column_recv.at[j, z_order[n]], buf.at[2 * r + j, pl.ds(2 * z_order[n], 2)])
-            plane(j, n, 0).start()
-            plane(j, n, 1).start()
-
-    def from_plane(j):
-        for n in range(2):
-            for way in range(2):
-                arrived(plane_recv.at[j, way, n], half_of(2 * (x_nbr, y_nbr)[way] + j, n))
-                if n == way:
-                    onward(j, way).start()
+    def own(j, n):
+        arrived(column_recv.at[j, z_order[n]], buf.at[2 * r + j, pl.ds(2 * z_order[n], 2)])
+        plane(j, n, 0).start()
+        plane(j, n, 1).start()
+
+    def from_plane(j, n):
+        for way in (n, 1 - n):
+            arrived(plane_recv.at[j, way, n], half_of(2 * (x_nbr, y_nbr)[way] + j, n))
+            if n == way:
+                onward(j, way).start()
 
     def from_diag(j):
         arrived(diag_recv.at[j], buf.at[2 * diag + j])
@@ -156,9 +197,9 @@
     dims = (((1,), (1,)), ((), ()))
     n_i = n_rep * rows
 
-    def to_core(t):
-        return pltpu.make_async_remote_copy(
-            src_ref=part.at[t, 1 - c], dst_ref=from_core.at[t], send_sem=core_send.at[t], recv_sem=core_recv.at[t],
+    def to_core(m):
+        return pltpu.make_async_remote_copy(
+            src_ref=part.at[m, 1 - c], dst_ref=from_core.at[m], send_sem=core_send.at[m], recv_sem=core_recv.at[m],
             device_id=(r, 2 * z + (1 - c)), device_id_type=MESH,
         )
 
@@ -173,63 +214,74 @@
         more = lax.dot_general(top, low[t], dims, preferred_element_type=jnp.float32)
         product = both[:n_i] + (both[n_i:] + more)
         for k in range(n_rep):
-            part[t, k % 2, k // 2] = product[k * rows:(k + 1) * rows]
-        to_core(t).start()
-
-    def to_z(t, k):
+            part[t // 2, k % 2, k // 2, t % 2] = product[k * rows:(k + 1) * rows]
+        if t % 2 == 1:
+            to_core(t // 2).start()
+
+    def to_z(m, k):
         there = (z + k) % 4
         return pltpu.make_async_remote_copy(
-            src_ref=summed.at[t, there], dst_ref=from_z.at[t, k - 1], send_sem=z_send.at[t, k - 1],
-            recv_sem=z_recv.at[t], device_id=(r, 2 * there + c), device_id_type=MESH,
-        )
-
-    def send_z(t):
-        to_core(t).wait_recv()
-        summed[t] = part[t, c] + from_core[t]
-        for k in range(1, 4):
-            to_z(t, k).start()
-
-    def finish(t):
-        arrived(z_recv.at[t], from_z.at[t])
-        total = (summed[t, z] + from_z[t, 0]) + (from_z[t, 1] + from_z[t, 2])
-        out[sym[t]] = 0.5 * total
-
-    relay(0)
-    relay(1)
+            src_ref=summed.at[m, there], dst_ref=from_z.at[m, k - 1], send_sem=z_send.at[m, k - 1],
+            recv_sem=z_recv.at[m], device_id=(r, 2 * there + c), device_id_type=MESH,
+        )
+
+    def send_z(m):
+        to_core(m).wait_recv()
+        summed[m] = part[m, c] + from_core[m]
+        for k in (2, 1, 3):
+            to_z(m, k).start()
+
+    def finish(m):
+        arrived(z_recv.at[m], from_z.at[m])
+        for j in range(2):
+            total = (summed[m, z, j] + from_z[m, 0, j]) + (from_z[m, 1, j] + from_z[m, 2, j])
+            out[sym[2 * m + j]] = 0.5 * total
+
     split(0)
+    hear(0)
+    tell(1)
     split(1)
-    own(0)
+    hear(1)
+    for j in range(2):
+        column_all(j, 0, start)
     split(2)
     split(3)
-    own(1)
+    split(4)
+    relay(0)
+    own(0,0)
+    own(0,1)
+    relay(1)
+    own(0,2)
+    own(0,3)
+    own(1,0)
+    own(1,1)
+    own(1,2)
+    own(1,3)
     multiply(0)
+    from_plane(0,0)
     multiply(1)
-    split(4)
-    from_plane(0)
+    from_plane(0,1)
+    split(5)
     send_z(0)
+    multiply(2)
+    from_plane(1,0)
+    multiply(3)
+    from_plane(1,1)
+    split(6)
+    split(7)
     send_z(1)
-    multiply(2)
-    multiply(3)
-    split(5)
-    from_plane(1)
-    send_z(2)
-    send_z(3)
     multiply(4)
     multiply(5)
-    split(6)
-    split(7)
-    send_z(4)
-    send_z(5)
+    send_z(2)
     from_diag(0)
     multiply(6)
     from_diag(1)
     multiply(7)
-    send_z(6)
-    for t in range(4):
-        finish(t)
-    send_z(7)
-    for t in range(4, 8):
-        finish(t)
+    finish(0)
+    finish(1)
+    send_z(3)
+    finish(2)
+    finish(3)
 
     for j in range(2):
         for k in range(1, 4):
@@ -240,10 +292,10 @@
             for n in range(4):
                 plane(j, n, way).wait_send()
             onward(j, way).wait_send()
-    for t in range(8):
-        to_core(t).wait_send()
+    for m in range(4):
+        to_core(m).wait_send()
         for k in range(1, 4):
-            to_z(t, k).wait_send()
+            to_z(m, k).wait_send()
 
 
 def per_device_kernel(amplitudes, integrals):
@@ -263,10 +315,10 @@
             pltpu.VMEM((n_sym, n_a, cols), bf16),
             pltpu.VMEM((2, 3, rows, amplitudes.shape[2]), f32),
             pltpu.VMEM((n_sym, n_rep, rows, cols), f32),
-            pltpu.VMEM((n_sym, 2, n_rep // 2, rows, n_a), f32),
-            pltpu.VMEM((n_sym, n_rep // 2, rows, n_a), f32),
-            pltpu.VMEM((n_sym, n_rep // 2, rows, n_a), f32),
-            pltpu.VMEM((n_sym, n_rep // 2 - 1, rows, n_a), f32),
+            pltpu.VMEM((n_sym // 2, 2, n_rep // 2, 2, rows, n_a), f32),
+            pltpu.VMEM((n_sym // 2, n_rep // 2, 2, rows, n_a), f32),
+            pltpu.VMEM((n_sym // 2, n_rep // 2, 2, rows, n_a), f32),
+            pltpu.VMEM((n_sym // 2, n_rep // 2 - 1, 2, rows, n_a), f32),
             dma((8,)),
             dma((2, 3)),
             dma((2, 3)),
@@ -276,10 +328,11 @@
             dma((2, 2, 2)),
             dma((2, 2)),
             dma((2,)),
-            dma((8,)),
-            dma((8,)),
-            dma((8, 3)),
-            dma((8,)),
+            dma((4,)),
+            dma((4,)),
+            dma((4, 3)),
+            dma((4,)),
+            pltpu.SemaphoreType.REGULAR((2,)),
         ],
         compiler_params=pltpu.CompilerParams(
             collective_id=0, has_side_effects=True, vmem_limit_bytes=48 * 2**20

time: 32.7 us -> 32.4 us (level)
    pallas_call x1, Pallas kernels: 31 us -> 30.7 us  [per_device_kernel(): pl.pallas_call(ladder_kernel, out_shape=jax.ShapeDtypeStruct((n_sym, rows...]
where the time goes in v3:
time: 32.4 us; the launch traced here: 32.3 us
  Pallas kernels  30.7 us (95%)
  local copies, waits for them, and re-layouts  1.58 us (5%)
    pallas_call x1, Pallas kernels, per_device_kernel(): pl.pallas_call(ladder_kernel, out_shape=jax.ShapeDtypeStruct((n_sym, rows...  30.7 us
    unnamed x3, local copies, waits for them, and re-layouts  1.58 us

profile of v3, /device:TPU:0, one launch (start us, length us, event | category | flops | bytes accessed | tf_op | source)
XLA Modules:
  0.0 32.3 jit_solution(8971721765456570562)
XLA Ops:
  0.0 0.0 copy-start
  0.0 0.9 %copy-done = f32[8,4,2048]{2,1,0:T(4,128)S(1)} copy-done((f32[8,4,2048]{2,1,0:T(4,128)S(1)}, f32[8,4,2048]{2,1,0:T(4,128)}, u32[]{:S(2)}) %copy-start) | copy-done | bytes 262168
  1.0 30.7 %shard_map.28 = f32[8,4,512]{2,1,0:T(4,128)S(1)} custom-call(f32[8,4,2048]{2,1,0:T(4,128)S(1)} %copy-done, f32[8,512,1024]{2,1,0:T(8,128)} %integ.1), custom_call_target="tpu_custom_call" | custom-call | flops 805306368 | bytes 16777216 | tf_op jit(solution)/shard_map/pallas_call | solution.py:307
  31.6 0.6 %copy.4 = f32[8,4,512]{2,1,0:T(4,128)} copy(f32[8,4,512]{2,1,0:T(4,128)S(1)} %shard_map.28) | data formatting | bytes 131072
Async XLA Ops:
  0.0 0.9 %copy-start = (f32[8,4,2048]{2,1,0:T(4,128)S(1)}, f32[8,4,2048]{2,1,0:T(4,128)}, u32[]{:S(2)}) copy-start(f32[8,4,2048]{2,1,0:T(4,128)} %amp.1) | copy-start | bytes 786436

commit v4 on v3

--- a/solution.py
+++ b/solution.py
@@ -23,9 +23,9 @@
 
 
 def ladder_kernel(
-    amp, integ, out,
-    raw, high, low, stage, buf, part, from_core, summed, from_z,
-    raw_sem, spread_send, spread_recv, column_send, column_recv, plane_send, plane_recv, diag_send, diag_recv,
+    amp_far, integ, out,
+    amp, raw, high, low, stage, buf, part, from_core, summed, from_z,
+    amp_sem, raw_sem, spread_send, spread_recv, column_send, column_recv, plane_send, plane_recv, diag_send, diag_recv,
     core_send, core_recv, z_send, z_recv, known,
 ):
     n_rep, rows, cols = buf.shape[1:]
@@ -42,6 +42,8 @@
     def load(t):
         return pltpu.make_async_copy(integ.at[sym[t]], raw.at[t], raw_sem.at[t])
 
+    fetch = pltpu.make_async_copy(amp_far, amp, amp_sem)
+    fetch.start()
     for t in range(8):
         load(t).start()
 
@@ -68,6 +70,7 @@
 
     inner = jnp.logical_and(has_below, has_above)
 
+    fetch.wait()
 
     @pl.when(inner)
     def _():
@@ -307,9 +310,10 @@
     return pl.pallas_call(
         ladder_kernel,
         out_shape=jax.ShapeDtypeStruct((n_sym, rows, n_a), f32),
-        in_specs=[pl.BlockSpec(memory_space=pl.ANY)] * 2,
+        in_specs=[pl.BlockSpec(memory_space=pltpu.HBM)] * 2,
         out_specs=pl.BlockSpec(memory_space=pltpu.VMEM),
         scratch_shapes=[
+            pltpu.VMEM(amplitudes.shape, f32),
             pltpu.VMEM((n_sym, n_a, cols), f32),
             pltpu.VMEM((n_sym, n_a, cols), bf16),
             pltpu.VMEM((n_sym, n_a, cols), bf16),
@@ -319,6 +323,7 @@
             pltpu.VMEM((n_sym // 2, n_rep // 2, 2, rows, n_a), f32),
             pltpu.VMEM((n_sym // 2, n_rep // 2, 2, rows, n_a), f32),
             pltpu.VMEM((n_sym // 2, n_rep // 2 - 1, 2, rows, n_a), f32),
+            dma,
             dma((8,)),
             dma((2, 3)),
             dma((2, 3)),

time: 32.4 us -> 32.5 us (level)
  no operation moved by 1% of the time
where the time goes in v4:
time: 32.5 us; the launch traced here: 32.3 us
  Pallas kernels  30.7 us (94%)
  local copies, waits for them, and re-layouts  1.58 us (5%)
    pallas_call x1, Pallas kernels, per_device_kernel(): pl.pallas_call(ladder_kernel, out_shape=jax.ShapeDtypeStruct((n_sym, rows...  30.7 us
    unnamed x3, local copies, waits for them, and re-layouts  1.58 us

profile of v4, /device:TPU:0, one launch (start us, length us, event | category | flops | bytes accessed | tf_op | source)
XLA Modules:
  0.0 32.3 jit_solution(13829637456140398526)
XLA Ops:
  0.0 0.0 copy-start
  0.0 0.9 %copy-done = f32[8,4,2048]{2,1,0:T(4,128)S(1)} copy-done((f32[8,4,2048]{2,1,0:T(4,128)S(1)}, f32[8,4,2048]{2,1,0:T(4,128)}, u32[]{:S(2)}) %copy-start) | copy-done | bytes 262168
  1.0 30.7 %shard_map.28 = f32[8,4,512]{2,1,0:T(4,128)S(1)} custom-call(f32[8,4,2048]{2,1,0:T(4,128)S(1)} %copy-done, f32[8,512,1024]{2,1,0:T(8,128)} %integ.1), custom_call_target="tpu_custom_call" | custom-call | flops 805306368 | bytes 16777216 | tf_op jit(solution)/shard_map/pallas_call | solution.py:310
  31.7 0.6 %copy.4 = f32[8,4,512]{2,1,0:T(4,128)} copy(f32[8,4,512]{2,1,0:T(4,128)S(1)} %shard_map.28) | data formatting | bytes 131072
Async XLA Ops:
  0.0 0.9 %copy-start = (f32[8,4,2048]{2,1,0:T(4,128)S(1)}, f32[8,4,2048]{2,1,0:T(4,128)}, u32[]{:S(2)}) copy-start(f32[8,4,2048]{2,1,0:T(4,128)} %amp_far.1) | copy-start | bytes 786436

commit v5 on v3

--- a/solution.py
+++ b/solution.py
@@ -248,9 +248,11 @@
     split(3)
     split(4)
     relay(0)
+    split(5)
     own(0,0)
     own(0,1)
     relay(1)
+    split(6)
     own(0,2)
     own(0,3)
     own(1,0)
@@ -258,17 +260,15 @@
     own(1,2)
     own(1,3)
     multiply(0)
+    split(7)
     from_plane(0,0)
     multiply(1)
     from_plane(0,1)
-    split(5)
     send_z(0)
     multiply(2)
     from_plane(1,0)
     multiply(3)
     from_plane(1,1)
-    split(6)
-    split(7)
     send_z(1)
     multiply(4)
     multiply(5)

time: 32.4 us -> 32.7 us (level)
    pallas_call x1, Pallas kernels: 30.7 us -> 31 us  [per_device_kernel(): pl.pallas_call(ladder_kernel, out_shape=jax.ShapeDtypeStruct((n_sym, rows...]
where the time goes in v5:
time: 32.7 us; the launch traced here: 32.6 us
  Pallas kernels  31 us (95%)
  local copies, waits for them, and re-layouts  1.58 us (5%)
    pallas_call x1, Pallas kernels, per_device_kernel(): pl.pallas_call(ladder_kernel, out_shape=jax.ShapeDtypeStruct((n_sym, rows...  31 us
    unnamed x3, local copies, waits for them, and re-layouts  1.58 us

profile of v5, /device:TPU:0, one launch (start us, length us, event | category | flops | bytes accessed | tf_op | source)
XLA Modules:
  0.0 32.6 jit_solution(15761925547068667263)
XLA Ops:
  0.0 0.0 copy-start
  0.0 0.9 %copy-done = f32[8,4,2048]{2,1,0:T(4,128)S(1)} copy-done((f32[8,4,2048]{2,1,0:T(4,128)S(1)}, f32[8,4,2048]{2,1,0:T(4,128)}, u32[]{:S(2)}) %copy-start) | copy-done | bytes 262168
  1.0 31.0 %shard_map.28 = f32[8,4,512]{2,1,0:T(4,128)S(1)} custom-call(f32[8,4,2048]{2,1,0:T(4,128)S(1)} %copy-done, f32[8,512,1024]{2,1,0:T(8,128)} %integ.1), custom_call_target="tpu_custom_call" | custom-call | flops 805306368 | bytes 16777216 | tf_op jit(solution)/shard_map/pallas_call | solution.py:307
  32.0 0.6 %copy.4 = f32[8,4,512]{2,1,0:T(4,128)} copy(f32[8,4,512]{2,1,0:T(4,128)S(1)} %shard_map.28) | data formatting | bytes 131072
Async XLA Ops:
  0.0 0.9 %copy-start = (f32[8,4,2048]{2,1,0:T(4,128)S(1)}, f32[8,4,2048]{2,1,0:T(4,128)}, u32[]{:S(2)}) copy-start(f32[8,4,2048]{2,1,0:T(4,128)} %amp.1) | copy-start | bytes 786436
